TPU v7x, 512 devices: a whole 4x8x8 slice. The times are simulated.
512 devices in a mesh: shot: 32 (over y, z_hi), point: 16 (over z_lo, x, core).
Axes of the slice: x: 4, y: 8, z: 8 (z_hi: 4, z_lo: 2; z = z_hi * 2 + z_lo), core: 2. Of those that a mesh axis runs over, the one named last changes fastest.
Arguments:
- traces: bfloat16 [64, 32, 1024], P('shot', 'point'), may hold values from -6 to 6
- panels: bfloat16 [32, 256, 1024], P('point', 'shot'), may hold values from -0.09375 to 0.09375
- aperture: int32 [64, 32], P('shot', 'point'), may hold values 0 or 1
- window_lo: int32 [256, 64], P('point', 'shot'), may hold values from 0 to 255
- window_hi: int32 [256, 64], P('point', 'shot'), may hold values from 512 to 1023
Outputs:
- multiples: bfloat16 [256, 64, 1024], P('point', 'shot')
All inputs are finite; a program needn't handle non-finite values. No bound on the sum of `aperture` on one device may be relied on, other than what follows from the above.
Results may differ from a plain program's by a relative error of at most 0.001.
Values may be sent and summed in bfloat16 or wider, within the bound.
A program may use at most 64 MiB of HBM per device.

v0:
```python
import jax
import jax.numpy as jnp
from jax import lax
from jax.sharding import PartitionSpec as P


def toeplitz(series):
    count = series.shape[-1]
    padded = jnp.concatenate([series, jnp.zeros_like(series)], -1)
    tiled_flat = jnp.tile(padded, (1, count))[:, : count * (2 * count - 1)]
    return tiled_flat.reshape(series.shape[0], count, 2 * count - 1)[:, :, :count]


def window_weights(window_lo, window_hi, length):
    sample_axis = jnp.arange(length).astype(jnp.float32)[None, None, :]
    lower = window_lo.astype(jnp.float32)[:, :, None]
    upper = window_hi.astype(jnp.float32)[:, :, None]
    rising = jnp.clip((sample_axis - lower + 32.0) / 32.0, 0.0, 1.0)
    falling = jnp.clip((upper - sample_axis) / 32.0, 0.0, 1.0)
    return rising * falling


def body(traces, panels, aperture, window_lo, window_hi):
    masked = traces * aperture[:, :, None].astype(traces.dtype)
    local_points = masked.shape[1]

    def kernel_maker():

        def kernel_for(point):
            return toeplitz(lax.dynamic_index_in_dim(masked, point, 1, keepdims=False))

        return kernel_for

    def make_convolve(kernel_for):

        def convolve(panel_piece, first_row):

            def one_point(point, total_sum):
                panel_rows = lax.dynamic_index_in_dim(panel_piece, point, 0, keepdims=False)
                return total_sum + jnp.einsum(
                    "ru,sut->rst", panel_rows, kernel_for(point), preferred_element_type=jnp.float32
                )

            initial = jnp.zeros(
                (panel_piece.shape[1], masked.shape[0], masked.shape[2]), jnp.float32
            )
            return lax.fori_loop(0, local_points, one_point, initial)

        return convolve

    convolve = make_convolve(kernel_maker())
    partial_terms = convolve(lax.all_gather(panels, "shot", axis=1, tiled=True), jnp.int32(0))
    predicted = lax.psum_scatter(partial_terms, "point", scatter_dimension=0, tiled=True)
    weights = window_weights(window_lo, window_hi, traces.shape[2])
    return (weights * predicted).astype(jnp.bfloat16)


def solution(mesh):
    in_specs = (
        P("shot", "point", None),
        P("point", "shot", None),
        P("shot", "point"),
        P("point", "shot"),
        P("point", "shot"),
    )
    out_specs = P("point", "shot", None)
    return jax.shard_map(body, mesh=mesh, in_specs=in_specs, out_specs=out_specs, check_vma=False)
```

profile of v0, /device:TPU:1, one launch (start us, length us, event | category | flops | bytes accessed | tf_op | source)
XLA Modules:
  0.0 359.0 jit_solution(9905600033228501757)
XLA Ops:
  6.5 0.0 all-gather.2.cloned.1.call-start
  6.5 0.7 all-gather.2.cloned.1.call-update
  7.3 0.0 all-reduce.4.cloned.1.call-start
  7.3 0.7 convert_element_type.25
  8.0 0.1 copy.18
  8.1 0.8 copy_multiply_fusion
  8.9 87.5 %all-gather.2.cloned.1.call-done = bf16[2,256,1024]{2,1,0:T(8,128)(2,1)} async-done(((bf16[2,8,1024]{2,1,0:T(8,128)(2,1)}), bf16[2,256,1024]{2,1,0:T(8,128)(2,1)}) %all-gather.2.cloned.1.call-update) | async-done | bytes 1048592 | tf_op jit(solution)/shard_map/all_gather | solution.py:52
  96.4 117.5 %while.14 = (s32[]{:T(128)}, f32[256,2,1024]{2,0,1:T(8,128)S(1)}, bf16[2,256,1024]{2,1,0:T(8,128)(2,1)}, bf16[2,2,1024]{2,0,1:T(2,128)(2,1)S(1)}, s32[]{:T(128)}, /*index=5*/bf16[]{:T(256)}, s32[]{:T(128)}) while((s32[]{:T(128)}, f32[256,2,1024]{2,0,1:T(8,128)S(1)}, bf16[2,256,1024]{2,1,0:T(8,128)(2,1)}, ...), condition=%wide.region_1.2_spmd.clone, body=%wide.region_0.1_spmd.clone.sunk | while | flops 1074790400 | bytes 88609400 | solution.py:47
  96.4 1.1 broadcast_bitcast_fusion.2
  97.4 17.3 %copy.24 = bf16[1,2,1024,2048]{3,1,2,0:T(2,128)(2,1)S(1)} copy(bf16[1,2,1024,2048]{3,2,1,0:T(8,128)(2,1)S(1)} %broadcast_bitcast_fusion.2) | data formatting | bytes 16777216 | tf_op jit(solution)/shard_map/while
  114.8 7.2 %slice.25 = bf16[2,2096128]{1,0:T(2,128)(2,1)} slice(bf16[2,2097152]{1,0:T(2,128)(2,1)S(1)} %bitcast.18), slice={[0:2], [0:2096128]} | slice | bytes 16769024 | tf_op jit(solution)/shard_map/while/body/eval_jaxpr/slice | solution.py:10
  121.9 11.9 %reshape.26 = bf16[4192256]{0:T(1024)(128)(2,1)} reshape(bf16[2,2096128]{1,0:T(2,128)(2,1)} %slice.25) | data formatting | bytes 16769024 | tf_op jit(solution)/shard_map/while
  133.8 0.0 copy-start.2
  133.8 17.4 %reshape.27 = bf16[2,1024,2047]{2,1,0:T(8,128)(2,1)} reshape(bf16[4192256]{0:T(1024)(128)(2,1)} %reshape.26) | data formatting | bytes 16769024 | tf_op jit(solution)/shard_map/while/body/eval_jaxpr/reshape | solution.py:11
  151.2 0.0 copy-done.2
  151.2 3.9 %select_add_fusion.2 = f32[256,2,1024]{2,0,1:T(8,128)S(1)} fusion(f32[256,2,1024]{2,0,1:T(8,128)S(1)} %get-tuple-element.141, bf16[2,1024,2047]{2,1,0:T(8,128)(2,1)} %reshape.27, pred[]{:T(512)S(6)} %compare.4, bf16[2,256,1024]{2,1,0:T(8,128)(2,1)S(1)} %copy-done.2, s32[]{:T(128)} %get-tuple-element.140), kind=kOutput, calls=%fused_computation.3.clone.1 | convolution fusion | flops 1074790400 | bytes 8913409 | tf_op jit(solution)/shard_map/while/body/eval_jaxpr/ru,sut->rst/dot_general | solution.py:40
  155.2 1.1 broadcast_bitcast_fusion.2
  156.2 17.3 %copy.24 = bf16[1,2,1024,2048]{3,1,2,0:T(2,128)(2,1)S(1)} copy(bf16[1,2,1024,2048]{3,2,1,0:T(8,128)(2,1)S(1)} %broadcast_bitcast_fusion.2) | data formatting | bytes 16777216 | tf_op jit(solution)/shard_map/while
  173.6 7.2 %slice.25 = bf16[2,2096128]{1,0:T(2,128)(2,1)} slice(bf16[2,2097152]{1,0:T(2,128)(2,1)S(1)} %bitcast.18), slice={[0:2], [0:2096128]} | slice | bytes 16769024 | tf_op jit(solution)/shard_map/while/body/eval_jaxpr/slice | solution.py:10
  180.7 11.9 %reshape.26 = bf16[4192256]{0:T(1024)(128)(2,1)} reshape(bf16[2,2096128]{1,0:T(2,128)(2,1)} %slice.25) | data formatting | bytes 16769024 | tf_op jit(solution)/shard_map/while
  192.6 0.0 copy-start.2
  192.6 17.4 %reshape.27 = bf16[2,1024,2047]{2,1,0:T(8,128)(2,1)} reshape(bf16[4192256]{0:T(1024)(128)(2,1)} %reshape.26) | data formatting | bytes 16769024 | tf_op jit(solution)/shard_map/while/body/eval_jaxpr/reshape | solution.py:11
  210.0 0.0 copy-done.2
  210.0 3.9 %select_add_fusion.2 = f32[256,2,1024]{2,0,1:T(8,128)S(1)} fusion(f32[256,2,1024]{2,0,1:T(8,128)S(1)} %get-tuple-element.141, bf16[2,1024,2047]{2,1,0:T(8,128)(2,1)} %reshape.27, pred[]{:T(512)S(6)} %compare.4, bf16[2,256,1024]{2,1,0:T(8,128)(2,1)S(1)} %copy-done.2, s32[]{:T(128)} %get-tuple-element.140), kind=kOutput, calls=%fused_computation.3.clone.1 | convolution fusion | flops 1074790400 | bytes 8913409 | tf_op jit(solution)/shard_map/while/body/eval_jaxpr/ru,sut->rst/dot_general | solution.py:40
  213.9 2.9 copy.20
  216.8 0.0 copy-start
  216.8 0.0 copy-start.1
  216.8 0.0 all-reduce.4.cloned.1.call-update
  216.9 0.6 copy-done
  217.5 0.1 copy.16
  217.6 0.0 copy-done.1
  217.6 0.1 copy.17
  217.7 1.3 dynamic-slice
  219.6 130.8 %all-reduce.4.cloned.1.call-done = f32[256,2,1024]{2,1,0:T(2,128)} async-done(((f32[256,2,1024]{2,1,0:T(2,128)}), f32[256,2,1024]{2,1,0:T(2,128)}) %all-reduce.4.cloned.1.call-update) | async-done | bytes 2097168
  350.4 1.8 fusion.7
  (8 shorter events, 0.0 us)
Async XLA Ops:
  6.5 89.8 %all-gather.2.cloned.1.call-start = ((), (), s32[]{:S(2)}) async-start(), calls=%async_computation | async-start | bytes 1081344 | tf_op jit(solution)/shard_map/all_gather | solution.py:52
  7.3 343.1 %all-reduce.4.cloned.1.call-start = ((), (), s32[]{:S(2)}) async-start(), calls=%async_computation.1 | async-start | bytes 4194304
  133.8 17.4 %copy-start.2 = (bf16[2,256,1024]{2,1,0:T(8,128)(2,1)S(1)}, bf16[2,256,1024]{2,1,0:T(8,128)(2,1)}, u32[]{:S(2)}) copy-start(bf16[2,256,1024]{2,1,0:T(8,128)(2,1)} %get-tuple-element.149) | copy-start | bytes 3145732 | tf_op jit(solution)/shard_map/while
  192.6 17.4 %copy-start.2 = (bf16[2,256,1024]{2,1,0:T(8,128)(2,1)S(1)}, bf16[2,256,1024]{2,1,0:T(8,128)(2,1)}, u32[]{:S(2)}) copy-start(bf16[2,256,1024]{2,1,0:T(8,128)(2,1)} %get-tuple-element.149) | copy-start | bytes 3145732 | tf_op jit(solution)/shard_map/while
  216.8 0.7 copy-start
  216.8 0.8 copy-start.1
Sparse Core Ops, SparseCore 0:
  10.5 85.7 all-gather.1
  217.0 133.3 all-reduce.3
where the time goes:
time: 359 us
  waiting for transfers between devices  219 us (61%)
  local copies, waits for them, and re-layouts  115 us (32%)
  between operations  14.1 us (4%)
  matrix products  7.74 us (2%)
    unnamed x3, waiting for transfers between devices  131 us
    all_gather x1, waiting for transfers between devices, body(): lax.all_gather(panels, 'shot', axis=1, tiled=True)  87.5 us
    while x10, local copies, waits for them, and re-layouts  60.6 us
    reshape x2, local copies, waits for them, and re-layouts, toeplitz(): tiled_flat.reshape(series.shape[0], count, 2 * count - 1)[:, :, :count]  34.8 us
    slice x2, local copies, waits for them, and re-layouts, toeplitz(): tiled_flat = jnp.tile(padded, (1, count))[:, :count * (2 * count - 1)]  14.3 us
    dot_general x2, matrix products, one_point(): jnp.einsum('ru,sut->rst', panel_rows, kernel_for(point), preferred_elemen...  7.74 us
  transfers between devices with their start and end apart: 2, of which 2 were waited for; matrix products, arithmetic and copies ran while one was open for 1% of the time, Pallas kernels for 0%

commit v1 on v0

--- a/solution.py
+++ b/solution.py
@@ -49,7 +49,12 @@
         return convolve
 
     convolve = make_convolve(kernel_maker())
-    partial_terms = convolve(lax.all_gather(panels, "shot", axis=1, tiled=True), jnp.int32(0))
+    partial_terms = convolve(
+        jnp.concatenate(
+            lax.all_to_all(jnp.stack([panels] * lax.axis_size("shot")), "shot", 0, 0), axis=1
+        ),
+        jnp.int32(0),
+    )
     predicted = lax.psum_scatter(partial_terms, "point", scatter_dimension=0, tiled=True)
     weights = window_weights(window_lo, window_hi, traces.shape[2])
     return (weights * predicted).astype(jnp.bfloat16)

time: 359 us -> 314 us (0.87)
  waiting for transfers between devices: 219 us -> 155 us
  starting transfers between devices: 0.04 us -> 16.5 us
    all_gather x1 -> x0, waiting for transfers between devices: 87.5 us -> none  [body(): lax.all_gather(panels, 'shot', axis=1, tiled=True)]
    all_to_all x0 -> x1, waiting for transfers between devices: none -> 27.2 us  [body(): lax.all_to_all(jnp.stack([panels] * lax.axis_size('shot')), 'shot', 0, 0)]
    all_to_all x0 -> x1, starting transfers between devices: none -> 16.5 us  [body(): lax.all_to_all(jnp.stack([panels] * lax.axis_size('shot')), 'shot', 0, 0)]
    unnamed x3 -> x2, waiting for transfers between devices: 131 us -> 128 us
where the time goes in v1:
time: 314 us
  waiting for transfers between devices  155 us (49%)
  local copies, waits for them, and re-layouts  118 us (38%)
  starting transfers between devices  16.5 us (5%)
  between operations  14.1 us (4%)
  matrix products  7.72 us (2%)
    unnamed x2, waiting for transfers between devices  128 us
    while x10, local copies, waits for them, and re-layouts  60.6 us
    reshape x2, local copies, waits for them, and re-layouts, toeplitz(): tiled_flat.reshape(series.shape[0], count, 2 * count - 1)[:, :, :count]  34.8 us
    all_to_all x1, waiting for transfers between devices, body(): lax.all_to_all(jnp.stack([panels] * lax.axis_size('shot')), 'shot', 0, 0)  27.2 us
    all_to_all x1, starting transfers between devices, body(): lax.all_to_all(jnp.stack([panels] * lax.axis_size('shot')), 'shot', 0, 0)  16.5 us
    slice x2, local copies, waits for them, and re-layouts, toeplitz(): tiled_flat = jnp.tile(padded, (1, count))[:, :count * (2 * count - 1)]  14.3 us
    dot_general x2, matrix products, one_point(): jnp.einsum('ru,sut->rst', panel_rows, kernel_for(point), preferred_elemen...  7.72 us
  transfers between devices with their start and end apart: 2, of which 2 were waited for; matrix products, arithmetic and copies ran while one was open for 1% of the time, Pallas kernels for 0%

profile of v1, /device:TPU:1, one launch (start us, length us, event | category | flops | bytes accessed | tf_op | source)
XLA Modules:
  0.0 313.6 jit_solution(5359845107617854949)
XLA Ops:
  6.5 0.0 copy-start.4
  6.5 0.0 copy-start.1
  6.5 1.9 stack.2
  8.4 16.5 %all-to-all-start = ((bf16[32,2,8,1024]{3,2,1,0:T(8,128)(2,1)}), bf16[32,2,8,1024]{3,2,1,0:T(8,128)(2,1)S(1)}, u32[]{:S(2)}, u32[]{:S(2)}) async-start(bf16[32,2,8,1024]{3,2,1,0:T(8,128)(2,1)} %stack.2), calls=%async_computation | async-start | bytes 2097152 | tf_op jit(solution)/shard_map/all_to_all | solution.py:54
  24.9 0.0 all-reduce.4.cloned.1.call-start
  25.0 0.0 copy-done.4
  25.0 0.1 copy.24
  25.1 0.0 copy-done.1
  25.1 0.1 copy_multiply_fusion
  25.2 27.2 %all-to-all-done = bf16[32,2,8,1024]{3,2,1,0:T(8,128)(2,1)S(1)} async-done(((bf16[32,2,8,1024]{3,2,1,0:T(8,128)(2,1)}), bf16[32,2,8,1024]{3,2,1,0:T(8,128)(2,1)S(1)}, u32[]{:S(2)}, u32[]{:S(2)}) %all-to-all-start) | async-done | bytes 1048608 | tf_op jit(solution)/shard_map/all_to_all | solution.py:54
  52.4 1.1 copy.30
  53.5 117.5 %while.14 = (s32[]{:T(128)}, f32[256,2,1024]{2,0,1:T(8,128)S(1)}, bf16[2,256,1024]{2,1,0:T(8,128)(2,1)}, bf16[2,2,1024]{2,0,1:T(2,128)(2,1)S(1)}, s32[]{:T(128)}, /*index=5*/bf16[]{:T(256)}, s32[]{:T(128)}) while((s32[]{:T(128)}, f32[256,2,1024]{2,0,1:T(8,128)S(1)}, bf16[2,256,1024]{2,1,0:T(8,128)(2,1)}, ...), condition=%wide.region_1.2_spmd.clone, body=%wide.region_0.1_spmd.clone.sunk | while | flops 1074790400 | bytes 88609400 | solution.py:47
  53.5 1.1 broadcast_bitcast_fusion.2
  54.6 17.3 %copy.32 = bf16[1,2,1024,2048]{3,1,2,0:T(2,128)(2,1)S(1)} copy(bf16[1,2,1024,2048]{3,2,1,0:T(8,128)(2,1)S(1)} %broadcast_bitcast_fusion.2) | data formatting | bytes 16777216 | tf_op jit(solution)/shard_map/while
  71.9 7.2 %slice.25 = bf16[2,2096128]{1,0:T(2,128)(2,1)} slice(bf16[2,2097152]{1,0:T(2,128)(2,1)S(1)} %bitcast.23), slice={[0:2], [0:2096128]} | slice | bytes 16769024 | tf_op jit(solution)/shard_map/while/body/eval_jaxpr/slice | solution.py:10
  79.1 11.9 %reshape.36 = bf16[4192256]{0:T(1024)(128)(2,1)} reshape(bf16[2,2096128]{1,0:T(2,128)(2,1)} %slice.25) | data formatting | bytes 16769024 | tf_op jit(solution)/shard_map/while
  91.0 0.0 copy-start
  91.0 17.4 %reshape.37 = bf16[2,1024,2047]{2,1,0:T(8,128)(2,1)} reshape(bf16[4192256]{0:T(1024)(128)(2,1)} %reshape.36) | data formatting | bytes 16769024 | tf_op jit(solution)/shard_map/while/body/eval_jaxpr/reshape | solution.py:11
  108.4 0.0 copy-done
  108.4 3.9 %select_add_fusion.2 = f32[256,2,1024]{2,0,1:T(8,128)S(1)} fusion(f32[256,2,1024]{2,0,1:T(8,128)S(1)} %get-tuple-element.141, bf16[2,1024,2047]{2,1,0:T(8,128)(2,1)} %reshape.37, pred[]{:T(512)S(6)} %compare.4, bf16[2,256,1024]{2,1,0:T(8,128)(2,1)S(1)} %copy-done, s32[]{:T(128)} %get-tuple-element.140), kind=kOutput, calls=%fused_computation.3.clone.1 | convolution fusion | flops 1074790400 | bytes 8913409 | tf_op jit(solution)/shard_map/while/body/eval_jaxpr/ru,sut->rst/dot_general | solution.py:40
  112.3 1.1 broadcast_bitcast_fusion.2
  113.4 17.3 %copy.32 = bf16[1,2,1024,2048]{3,1,2,0:T(2,128)(2,1)S(1)} copy(bf16[1,2,1024,2048]{3,2,1,0:T(8,128)(2,1)S(1)} %broadcast_bitcast_fusion.2) | data formatting | bytes 16777216 | tf_op jit(solution)/shard_map/while
  130.7 7.2 %slice.25 = bf16[2,2096128]{1,0:T(2,128)(2,1)} slice(bf16[2,2097152]{1,0:T(2,128)(2,1)S(1)} %bitcast.23), slice={[0:2], [0:2096128]} | slice | bytes 16769024 | tf_op jit(solution)/shard_map/while/body/eval_jaxpr/slice | solution.py:10
  137.9 11.9 %reshape.36 = bf16[4192256]{0:T(1024)(128)(2,1)} reshape(bf16[2,2096128]{1,0:T(2,128)(2,1)} %slice.25) | data formatting | bytes 16769024 | tf_op jit(solution)/shard_map/while
  149.8 0.0 copy-start
  149.8 17.4 %reshape.37 = bf16[2,1024,2047]{2,1,0:T(8,128)(2,1)} reshape(bf16[4192256]{0:T(1024)(128)(2,1)} %reshape.36) | data formatting | bytes 16769024 | tf_op jit(solution)/shard_map/while/body/eval_jaxpr/reshape | solution.py:11
  167.2 0.0 copy-done
  167.2 3.9 %select_add_fusion.2 = f32[256,2,1024]{2,0,1:T(8,128)S(1)} fusion(f32[256,2,1024]{2,0,1:T(8,128)S(1)} %get-tuple-element.141, bf16[2,1024,2047]{2,1,0:T(8,128)(2,1)} %reshape.37, pred[]{:T(512)S(6)} %compare.4, bf16[2,256,1024]{2,1,0:T(8,128)(2,1)S(1)} %copy-done, s32[]{:T(128)} %get-tuple-element.140), kind=kOutput, calls=%fused_computation.3.clone.1 | convolution fusion | flops 1074790400 | bytes 8913409 | tf_op jit(solution)/shard_map/while/body/eval_jaxpr/ru,sut->rst/dot_general | solution.py:40
  171.0 2.9 copy.26
  174.0 0.0 copy-start.2
  174.0 0.0 copy-start.3
  174.0 0.0 all-reduce.4.cloned.1.call-update
  174.0 0.6 copy-done.2
  174.6 0.1 copy.21
  174.7 0.0 copy-done.3
  174.7 0.1 copy.22
  174.8 1.3 dynamic-slice
  176.8 128.2 %all-reduce.4.cloned.1.call-done = f32[256,2,1024]{2,1,0:T(2,128)} async-done(((f32[256,2,1024]{2,1,0:T(2,128)}), f32[256,2,1024]{2,1,0:T(2,128)}) %all-reduce.4.cloned.1.call-update) | async-done | bytes 2097168
  304.9 1.8 fusion.7
  (9 shorter events, 0.1 us)
Async XLA Ops:
  6.5 18.5 %copy-start.4 = (s32[2,2]{1,0:T(2,128)S(1)}, s32[2,2]{1,0:T(2,128)}, u32[]{:S(2)}) copy-start(s32[2,2]{1,0:T(2,128)} %param.9) | copy-start | bytes 52
  6.5 18.6 %copy-start.1 = (bf16[2,2,1024]{2,1,0:T(2,128)(2,1)S(1)}, bf16[2,2,1024]{2,1,0:T(2,128)(2,1)}, u32[]{:S(2)}) copy-start(bf16[2,2,1024]{2,1,0:T(2,128)(2,1)} %param.7) | copy-start | bytes 24580
  8.4 44.0 %all-to-all-start = ((bf16[32,2,8,1024]{3,2,1,0:T(8,128)(2,1)}), bf16[32,2,8,1024]{3,2,1,0:T(8,128)(2,1)S(1)}, u32[]{:S(2)}, u32[]{:S(2)}) async-start(bf16[32,2,8,1024]{3,2,1,0:T(8,128)(2,1)} %stack.2), calls=%async_computation | async-start | bytes 2097152 | tf_op jit(solution)/shard_map/all_to_all | solution.py:54
  24.9 280.0 %all-reduce.4.cloned.1.call-start = ((), (), s32[]{:S(2)}) async-start(), calls=%async_computation.1 | async-start | bytes 4194304
  91.0 17.4 %copy-start = (bf16[2,256,1024]{2,1,0:T(8,128)(2,1)S(1)}, bf16[2,256,1024]{2,1,0:T(8,128)(2,1)}, u32[]{:S(2)}) copy-start(bf16[2,256,1024]{2,1,0:T(8,128)(2,1)} %get-tuple-element.149) | copy-start | bytes 3145732 | tf_op jit(solution)/shard_map/while
  149.8 17.4 %copy-start = (bf16[2,256,1024]{2,1,0:T(8,128)(2,1)S(1)}, bf16[2,256,1024]{2,1,0:T(8,128)(2,1)}, u32[]{:S(2)}) copy-start(bf16[2,256,1024]{2,1,0:T(8,128)(2,1)} %get-tuple-element.149) | copy-start | bytes 3145732 | tf_op jit(solution)/shard_map/while
  174.0 0.7 copy-start.2
  174.0 0.8 copy-start.3
Sparse Core Ops, SparseCore 0:
  174.1 130.7 all-reduce.3
